TPU v7x, 32 devices: a whole 2x2x4 slice. The times are simulated.
32 devices in a mesh: groups: 2 (over y), wide: 4 (over z), pair: 2 (over x), cores: 2 (over core).
Axes of the slice: x: 2, y: 2, z: 4, core: 2. Of those that a mesh axis runs over, the one named last changes fastest.
Arguments:
- layer_input: bfloat16 [256, 30, 256], P(('groups', 'wide', 'pair', 'cores')), parts along dimension 0, may hold values from -6 to 6
- mixed_heads: bfloat16 [256, 30, 256], P(('groups', 'wide', 'pair', 'cores')), parts along dimension 0, may hold values from -6 to 6
- cotangents: bfloat16 [256, 4, 30, 256], P(('groups', 'wide', 'pair', 'cores')), parts along dimension 0, may hold values from -0.00012207031 to 0.00012207031
- local_energy: float32 [256], P(('groups', 'wide', 'pair', 'cores')), parts along dimension 0, may hold values from -6 to 6
Outputs:
- update: float32 [2048, 256], P(('groups', 'wide', 'pair', 'cores')), parts along dimension 0
There are 2 independent parts, one for each index of `groups`. A program takes and returns all parts, laid end to end along the dimension named above; each array names one. Nothing has to cross between parts.
All inputs are finite; a program needn't handle non-finite values.
Results may differ from a plain program's by a relative error of at most 0.005.
Values may be sent and summed in bfloat16 or wider, within the bound.
A program may use at most 128 MiB of HBM per device.

v0:
```python
import math

import jax
import jax.numpy as jnp
from jax import lax
from jax.sharding import PartitionSpec as P


def solve_damped(damped, right_side):
    lower = jnp.linalg.cholesky(damped)
    forward = jax.scipy.linalg.solve_triangular(lower, right_side, lower=True)
    return jax.scipy.linalg.solve_triangular(lower, forward, lower=True, trans=1)


def body(layer_input, mixed_heads, cotangents, local_energy):
    lanes = lax.axis_size(("wide", "pair", "cores"))
    walk_dev = layer_input.shape[0]
    width = layer_input.shape[2]
    walkers = walk_dev * lanes
    inv_root = 1.0 / math.sqrt(walkers)
    three = jnp.einsum(
        "wei,wmej->wmij", layer_input, cotangents[:, :3], preferred_element_type=jnp.float32
    )
    last = jnp.einsum(
        "wei,wej->wij", mixed_heads, cotangents[:, 3], preferred_element_type=jnp.float32
    )
    grads = jnp.concatenate(
        [three.astype(jnp.bfloat16).reshape(walk_dev, 3 * width, width), last.astype(jnp.bfloat16)],
        axis=1,
    )
    regrouped = lax.all_to_all(
        grads, ("wide", "pair", "cores"), split_axis=1, concat_axis=0, tiled=True
    )
    rows_dev = regrouped.shape[1]
    flattened = regrouped.reshape(walkers, rows_dev * width)
    average = jnp.mean(flattened, axis=0, dtype=jnp.float32)
    centered = ((flattened.astype(jnp.float32) - average) * inv_root).astype(jnp.bfloat16)
    energies = lax.all_gather(local_energy, ("wide", "pair", "cores"), axis=0, tiled=True)
    partial_value = jnp.dot(centered, centered.T, preferred_element_type=jnp.float32)
    gram = lax.psum(partial_value, ("wide", "pair", "cores"))
    right_side = (energies - jnp.mean(energies)) * inv_root
    damped = gram + 0.01 * jnp.trace(gram) / walkers * jnp.eye(walkers, dtype=jnp.float32)
    coefficients = solve_damped(damped, right_side)
    weights = coefficients.astype(jnp.bfloat16)
    update = jnp.dot(weights, centered, preferred_element_type=jnp.float32)
    return update.reshape(rows_dev, width)


def solution(mesh):
    placed = (
        P(("groups", "wide", "pair", "cores"), None, None),
        P(("groups", "wide", "pair", "cores"), None, None),
        P(("groups", "wide", "pair", "cores"), None, None, None),
        P(("groups", "wide", "pair", "cores")),
    )
    return jax.shard_map(
        body,
        mesh=mesh,
        in_specs=placed,
        out_specs=P(("groups", "wide", "pair", "cores"), None),
        check_vma=False,
    )
```

profile of v0, /device:TPU:0, one launch (start us, length us, event | category | flops | bytes accessed | tf_op | source)
XLA Modules:
  0.0 271.7 jit_solution(17750342878656423521)
XLA Ops:
  6.5 0.0 copy-start
  6.5 1.3 slice.25
  7.9 0.0 copy-done
  7.9 0.0 copy-start.1
  7.9 2.1 convolution_convert_fusion
  10.0 1.8 copy.26
  11.8 0.0 copy-done.1
  11.8 0.5 convolution_convert_fusion.1
  12.3 0.6 copy.27
  12.9 2.3 pad_maximum_fusion
  15.2 0.0 copy-start.3
  15.2 0.0 copy-start.2
  15.2 7.5 %all-to-all-start = ((bf16[8,1024,256]{2,0,1:T(8,128)(2,1)}), bf16[8,1024,256]{2,0,1:T(8,128)(2,1)}, u32[]{:S(2)}, u32[]{:S(2)}) async-start(bf16[8,1024,256]{2,0,1:T(8,128)(2,1)} %pad_maximum_fusion), calls=%async_computation | async-start | bytes 8388608 | tf_op jit(solution)/shard_map/all_to_all | solution.py:31
  22.7 0.0 all-reduce.3.cloned.1.call-start
  22.8 0.0 copy-done.3
  22.8 0.6 dynamic-slice
  24.1 0.0 copy-done.2
  24.1 0.2 dynamic-update-slice.3
  24.3 94.9 %all-reduce = f32[128]{0:T(128)S(1)} all-reduce(f32[128]{0:T(128)S(1)} %dynamic-update-slice.3), channel_id=1, replica_groups=mesh['groups'=2,'wide'=4,'pair'=2,'cores'=2] {'wide','pair','cores'}, use_global_device_ids=true, to_apply=%add | all-reduce | flops 128 | bytes 1024
  119.2 0.6 reduce_sum.30
  120.4 0.0 all-to-all-done
  120.4 6.6 %convert_bitcast_fusion = (f32[16,8,64,256]{3,2,0,1:T(8,128)}, bf16[8,1024,256]{2,1,0:T(8,128)(2,1)S(1)}) fusion(bf16[8,1024,256]{2,0,1:T(8,128)(2,1)} %all-to-all-done), kind=kLoop, calls=%fused_computation | loop fusion | flops 2097152 | bytes 16777216 | tf_op jit(solution)/shard_map/convert_element_type | solution.py:37
  127.0 0.6 fusion
  127.7 3.2 %copy_bitcast_fusion.1 = bf16[16,8,64,256]{3,2,1,0:T(8,128)(2,1)S(1)} fusion(f32[64,256]{1,0:T(8,128)S(1)} %get-tuple-element.8, bf16[8,1024,256]{2,0,1:T(8,128)(2,1)} %all-to-all-done), kind=kLoop, calls=%fused_computation.9 | loop fusion | flops 8388608 | bytes 8454144
  130.9 2.9 %copy.40 = bf16[16,8,64,256]{3,1,2,0:T(8,128)(2,1)S(1)} copy(bf16[16,8,64,256]{3,2,1,0:T(8,128)(2,1)S(1)} %copy_bitcast_fusion.1) | data formatting | bytes 8388608
  133.7 1.9 fusion.20
  135.6 0.0 all-reduce.3.cloned.1.call-update
  135.7 4.0 %copy.62 = f32[16,8,64,256]{3,2,1,0:T(8,128)S(1)} copy(f32[16,8,64,256]{3,2,0,1:T(8,128)} %get-tuple-element.5) | data formatting | bytes 16777216 | tf_op jit(solution)/shard_map/convert_element_type | solution.py:37
  139.7 6.6 %copy.41 = f32[16,8,64,256]{3,1,2,0:T(8,128)S(1)} copy(f32[16,8,64,256]{3,2,1,0:T(8,128)S(1)} %copy.62) | data formatting | bytes 16777216
  146.3 3.0 %multiply_convert_fusion = bf16[128,16384]{1,0:T(8,128)(2,1)} fusion(f32[128,16384]{1,0:T(8,128)S(1)} %bitcast.72, f32[16384]{0:T(1024)S(1)} %bitcast.77), kind=kLoop, calls=%fused_computation.2 | loop fusion | flops 6291456 | bytes 12648448 | tf_op jit(solution)/shard_map/convert_element_type | solution.py:37
  149.3 84.9 %all-reduce.3.cloned.1.call-done = f32[128,128]{1,0:T(8,128)} async-done(((f32[128,128]{1,0:T(8,128)}), f32[128,128]{1,0:T(8,128)}) %all-reduce.3.cloned.1.call-update) | async-done | bytes 65552 | tf_op jit(solution)/shard_map/psum | solution.py:40
  234.1 1.5 select_reduce_fusion.1
  236.3 0.9 select_add_fusion
  237.1 0.1 copy.30
  237.2 0.9 fusion.12
  238.1 11.7 %cholesky.17 = f32[128,128]{1,0:T(8,128)S(1)} custom-call(f32[128,128]{1,0:T(8,128)S(1)} %fusion.12), custom_call_target="Cholesky" | custom-call | tf_op jit(solution)/shard_map/jit(cholesky)/cholesky | solution.py:10
  249.8 0.6 compare_reduce_fusion
  250.5 0.7 fusion.9
  251.1 9.8 %custom-call.10 = f32[1,128,128]{1,2,0:T(8,128)S(1)} custom-call(f32[1,128,128]{2,1,0:T(8,128)S(1)} %fusion.9), custom_call_target="InvertDiagBlocksLowerTriangular" | custom-call | tf_op jit(solution)/shard_map/jit(_solve_triangular)/triangular_solve | solution.py:12
  261.0 0.2 convolution_bitcast_fusion.1
  261.1 0.2 fusion.5
  261.3 2.9 %fusion.1 = f32[1,64,256]{2,0,1:T(1,128)S(1)} fusion(bf16[128,1,1]{0,1,2:T(2,128)(2,1)S(1)} %fusion.5, bf16[16,64,8,256]{3,2,1,0:T(8,128)(2,1)} %bitcast.73), kind=kOutput, calls=%fused_computation.5 | convolution fusion | flops 4194304 | bytes 4260096 | tf_op jit(solution)/shard_map/dot_general | solution.py:45
  264.2 0.6 copy.63
  (4 shorter events, 0.1 us)
Async XLA Ops:
  6.5 1.3 copy-start
  7.9 3.9 %copy-start.1 = (bf16[8,30,256]{2,0,1:T(8,128)(2,1)S(1)}, bf16[8,30,256]{2,0,1:T(8,128)(2,1)}, u32[]{:S(2)}) copy-start(bf16[8,30,256]{2,0,1:T(8,128)(2,1)} %param.5) | copy-start | bytes 368644
  15.2 7.6 %copy-start.3 = (u32[32]{0:T(128)S(1)}, u32[32]{0:T(128)}, u32[]{:S(2)}) copy-start(u32[32]{0:T(128)} %constant.73) | copy-start | bytes 388
  15.2 8.9 %copy-start.2 = (f32[8]{0:T(128)S(1)}, f32[8]{0:T(128)}, u32[]{:S(2)}) copy-start(f32[8]{0:T(128)} %param.7) | copy-start | bytes 100
  15.2 105.2 %all-to-all-start = ((bf16[8,1024,256]{2,0,1:T(8,128)(2,1)}), bf16[8,1024,256]{2,0,1:T(8,128)(2,1)}, u32[]{:S(2)}, u32[]{:S(2)}) async-start(bf16[8,1024,256]{2,0,1:T(8,128)(2,1)} %pad_maximum_fusion), calls=%async_computation | async-start | bytes 8388608 | tf_op jit(solution)/shard_map/all_to_all | solution.py:31
  22.7 211.4 %all-reduce.3.cloned.1.call-start = ((), (), s32[]{:S(2)}) async-start(), calls=%async_computation.1 | async-start | bytes 131072 | tf_op jit(solution)/shard_map/psum | solution.py:40
Sparse Core Ops, SparseCore 0:
  135.8 98.3 all-reduce.2
where the time goes:
time: 273 us; the launch traced here: 272 us
  blocking collectives  94.9 us (35%)
  waiting for transfers between devices  84.9 us (31%)
  other arithmetic  42.3 us (15%)
  local copies, waits for them, and re-layouts  18.8 us (7%)
  between operations  15.5 us (6%)
  matrix products  7.69 us (3%)
  starting transfers between devices  7.58 us (3%)
    unnamed x1, blocking collectives  94.9 us
    psum x1, waiting for transfers between devices, body(): gram = lax.psum(partial_value, ('wide', 'pair', 'cores'))  84.9 us
    another operation x3, other arithmetic, solve_damped(): lower = jnp.linalg.cholesky(damped)  12.4 us
    another operation x2, other arithmetic, solve_damped(): jax.scipy.linalg.solve_triangular(lower, forward, lower=True, trans=1)  10.5 us
    unnamed x14, local copies, waits for them, and re-layouts  10.4 us
    all_to_all x1, starting transfers between devices, body(): lax.all_to_all(grads, ('wide', 'pair', 'cores'), split_axis=1, concat_axi...  7.54 us
    convert_element_type x1, other arithmetic, body(): flattened.astype(jnp.float32) - average  6.63 us
  transfers between devices with their start and end apart: 2, of which 1 were waited for; matrix products, arithmetic and copies ran while one was open for 6% of the time, Pallas kernels for 0%

commit v1 on v0

v1 whole, which is shorter than its diff:
```python
import functools
import math

import jax
import jax.numpy as jnp
from jax import lax
from jax.experimental import pallas as pl
from jax.experimental.pallas import tpu as pltpu
from jax.sharding import PartitionSpec as P

MESH = pl.DeviceIdType.MESH
AXES = ("groups", "wide", "pair", "cores")


def solve_damped(damped, right_side):
    lower = jnp.linalg.cholesky(damped)
    forward = jax.scipy.linalg.solve_triangular(lower, right_side, lower=True)
    return jax.scipy.linalg.solve_triangular(lower, forward, lower=True, trans=1)


def gather_kernel(
    nz, nx, rows, elec, inv_root,
    c_ref, st_ref, en_ref, cent_ref, gall_ref,
    cbuf, sz, sx, sbuf, grads, gpart, rbuf, gbuf,
    zs_c, zr_c, zs_s, zr_s, xs_c, xr_c, xs_s, xr_s, cs_c, cr_c, cs_s, cr_s,
    gs, gr, hs, hr,
):
    g, z, x, c = (lax.axis_index(a) for a in AXES)
    nc = 2
    ndev = nz * nx * nc
    sib = 1 - c
    me = (z * nx + x) * nc + c
    used = c_ref.shape[1]
    depth = cbuf.shape[1]
    width = cbuf.shape[2]
    walk = ndev * 8

    def dev(d):
        return (g, d // (nx * nc), (d // nc) % nx, d % nc)

    def clear(o, unused):
        cbuf[o, used:depth, :] = jnp.zeros((depth - used, width), cbuf.dtype)
        return unused
    lax.fori_loop(0, ndev, clear, 0)

    barrier = pltpu.get_barrier_semaphore()

    def greet(k, unused):
        d = lax.rem(me + k, ndev)
        pl.semaphore_signal(barrier, inc=1, device_id=dev(d), device_id_type=MESH)
        return unused
    lax.fori_loop(1, ndev, greet, 0)
    pl.semaphore_wait(barrier, ndev - 1)

    def origin(s, xx, cc):
        return (s * nx + xx) * nc + cc

    def z_copies(zt, src_z, dz):
        m = (4 * zt) // nz
        o = origin(src_z, x, c)
        return (
            pltpu.make_async_remote_copy(
                c_ref.at[m], cbuf.at[o, pl.ds(0, used)], zs_c.at[dz], zr_c.at[src_z],
                device_id=(g, zt, x, c), device_id_type=MESH),
            pltpu.make_async_remote_copy(
                st_ref.at[pl.ds(zt * nx * nc, nx * nc)], sz.at[src_z], zs_s.at[dz], zr_s.at[src_z],
                device_id=(g, zt, x, c), device_id_type=MESH),
        )

    def x_copies(s, xo, xt, dx):
        o = origin(s, xo, c)
        return (
            pltpu.make_async_remote_copy(
                cbuf.at[o, pl.ds(0, used)], cbuf.at[o, pl.ds(0, used)], xs_c.at[dx, s], xr_c.at[xo, s],
                device_id=(g, z, xt, c), device_id_type=MESH),
            pltpu.make_async_remote_copy(
                sz.at[s, pl.ds(xt * nc, nc)], sx.at[xo, s], xs_s.at[dx, s], xr_s.at[xo, s],
                device_id=(g, z, xt, c), device_id_type=MESH),
        )

    def c_copies(s, xo, co, src):
        o = origin(s, xo, co)
        return (
            pltpu.make_async_remote_copy(
                cbuf.at[o, pl.ds(0, used)], cbuf.at[o, pl.ds(0, used)], cs_c.at[xo, s], cr_c.at[xo, s],
                device_id=(g, z, x, sib), device_id_type=MESH),
            pltpu.make_async_remote_copy(
                src, sbuf.at[o], cs_s.at[xo, s], cr_s.at[xo, s],
                device_id=(g, z, x, sib), device_id_type=MESH),
        )

    def z_send(dz, unused):
        for copy in z_copies(lax.rem(z + dz, nz), z, dz):
            copy.start()
        return unused
    lax.fori_loop(1, nz, z_send, 0)

    cbuf[me, 0:used, :] = c_ref[(4 * z) // nz]
    sz[z] = st_ref[pl.ds(z * nx * nc, nx * nc)]

    slot = lax.broadcasted_iota(jnp.int32, (8, depth), 1)
    walker = lax.broadcasted_iota(jnp.int32, (8, depth), 0)
    own = (slot >= walker * elec) & (slot < walker * elec + elec)
    step = min(rows, 16)

    def form(p):
        def part(k, unused):
            base = pl.multiple_of(k * step, step)
            halves = []
            for h in range(nc):
                piece = sbuf[p * nc + h, pl.ds(base, step), :].astype(jnp.float32)
                spread = jnp.where(own[None], piece[:, None, :], 0.0)
                left = spread.reshape(step * 8, depth).astype(jnp.bfloat16)
                out = jnp.dot(left, cbuf[p * nc + h], preferred_element_type=jnp.float32)
                halves.append(out.reshape(step, 8, width))
            both = jnp.concatenate(halves, axis=1).astype(jnp.bfloat16)
            grads[pl.ds(base, step), pl.ds(pl.multiple_of(p * 16, 16), 16), :] = both
            return unused
        lax.fori_loop(0, rows // step, part, 0)

    def pipeline(t, unused):
        @pl.when(t < nz)
        def first():
            s = lax.rem(z + nz - t, nz)

            @pl.when(t > 0)
            def arrived():
                for copy in z_copies(z, s, 0):
                    copy.wait_recv()
            for dx in range(1, nx):
                for copy in x_copies(s, x, lax.rem(x + dx, nx), dx):
                    copy.start()
            for copy in c_copies(s, x, c, sz.at[s, x * nc + sib]):
                copy.start()
            sbuf[origin(s, x, c)] = sz[s, x * nc + c]

        @pl.when((t >= 1) & (t < nz + 1))
        def second():
            s = lax.rem(z + nz - t + 1, nz)
            for dx in range(1, nx):
                xo = lax.rem(x + nx - dx, nx)
                for copy in x_copies(s, xo, x, 0):
                    copy.wait_recv()
                for copy in c_copies(s, xo, c, sx.at[xo, s, sib]):
                    copy.start()
                sbuf[origin(s, xo, c)] = sx[xo, s, c]

        @pl.when(t >= 2)
        def third():
            s = lax.rem(z + nz - t + 2, nz)
            for dx in range(nx):
                xo = lax.rem(x + nx - dx, nx)
                for copy in c_copies(s, xo, sib, sz.at[s, 0]):
                    copy.wait_recv()
                form(s * nx + xo)
        return unused
    lax.fori_loop(0, nz + 2, pipeline, 0)

    gpart[...] = jnp.zeros_like(gpart)
    batch = 4

    def share(k, unused):
        pieces = []
        for j in range(batch):
            stored = grads[k * batch + j].astype(jnp.float32)
            average = jnp.mean(stored, axis=0, keepdims=True)
            piece = ((stored - average) * inv_root).astype(jnp.bfloat16)
            cent_ref[k * batch + j] = piece
            pieces.append(piece)
        flat = jnp.concatenate(pieces, axis=1)
        for r in range(walk // 128):
            add = lax.dot_general(flat[r * 128:(r + 1) * 128], flat, (((1,), (1,)), ((), ())),
                                  preferred_element_type=jnp.float32)
            gpart[r * 16:(r + 1) * 16] += add.reshape(16, 8, walk)
        return unused
    lax.fori_loop(0, rows // batch, share, 0)

    def g_copy(src_d, dst_d, k):
        return pltpu.make_async_remote_copy(
            gpart.at[dst_d], rbuf.at[src_d], gs.at[k], gr.at[src_d], device_id=dev(dst_d), device_id_type=MESH)

    def h_copy(src_d, dst_d, k):
        return pltpu.make_async_remote_copy(
            gbuf.at[src_d], gbuf.at[src_d], hs.at[k], hr.at[src_d], device_id=dev(dst_d), device_id_type=MESH)

    def each(fn):
        def run(k, unused):
            fn(k)
            return unused
        lax.fori_loop(1, ndev, run, 0)

    each(lambda k: g_copy(me, lax.rem(me + k, ndev), k).start())
    rbuf[me] = gpart[me]
    each(lambda k: g_copy(lax.rem(me + k, ndev), me, k).wait_recv())
    gbuf[me, :, 0:walk] = jnp.sum(rbuf[...], axis=0)
    gbuf[me, :, walk:walk + 128] = en_ref[...]
    each(lambda k: h_copy(me, lax.rem(me + k, ndev), k).start())
    each(lambda k: h_copy(lax.rem(me + k, ndev), me, k).wait_recv())
    gall_ref[...] = gbuf[...]

    each(lambda k: g_copy(me, lax.rem(me + k, ndev), k).wait_send())
    each(lambda k: h_copy(me, lax.rem(me + k, ndev), k).wait_send())

    def z_left(dz, unused):
        for copy in z_copies(lax.rem(z + dz, nz), z, dz):
            copy.wait_send()
        return unused
    lax.fori_loop(1, nz, z_left, 0)

    def s_left(s, unused):
        for dx in range(1, nx):
            for copy in x_copies(s, x, lax.rem(x + dx, nx), dx):
                copy.wait_send()
        for xo in range(nx):
            for copy in c_copies(s, xo, c, sz.at[s, 0]):
                copy.wait_send()
        return unused
    lax.fori_loop(0, nz, s_left, 0)


def body(nz, nx, layer_input, mixed_heads, cotangents, local_energy):
    nc = 2
    ndev = nz * nx * nc
    walk_dev, elec, width = layer_input.shape
    walkers = walk_dev * ndev
    inv_root = 1.0 / math.sqrt(walkers)
    rows = 4 * width // ndev
    rows_held = max(rows, 16)
    used = walk_dev * elec
    depth = -(-used // 128) * 128

    def turned(source):
        return jnp.pad(source.reshape(used, width).T, ((0, 0), (0, depth - used)))

    layer = turned(layer_input)
    sources = jnp.concatenate([layer, layer, layer, turned(mixed_heads)], axis=0).reshape(ndev, rows, depth)
    sources = jnp.pad(sources, ((0, 0), (0, rows_held - rows), (0, 0)))
    cots = jnp.swapaxes(cotangents, 0, 1).reshape(4, used, width)
    energy = jnp.broadcast_to(local_energy[:, None], (walk_dev, 128))

    bf, f32 = jnp.bfloat16, jnp.float32
    dma = pltpu.SemaphoreType.DMA
    vmem = pl.BlockSpec(memory_space=pltpu.VMEM)
    centered, everything = pl.pallas_call(
        functools.partial(gather_kernel, nz, nx, rows, elec, inv_root),
        out_shape=(
            jax.ShapeDtypeStruct((rows, walkers, width), bf),
            jax.ShapeDtypeStruct((ndev, walk_dev, walkers + 128), f32),
        ),
        in_specs=[vmem] * 3,
        out_specs=(vmem, vmem),
        scratch_shapes=[
            pltpu.VMEM((ndev, depth, width), bf),
            pltpu.VMEM((nz, nx * nc, rows_held, depth), bf),
            pltpu.VMEM((nx, nz, nc, rows_held, depth), bf),
            pltpu.VMEM((ndev, rows_held, depth), bf),
            pltpu.VMEM((rows, walkers, width), bf),
            pltpu.VMEM((ndev, walk_dev, walkers), f32),
            pltpu.VMEM((ndev, walk_dev, walkers), f32),
            pltpu.VMEM((ndev, walk_dev, walkers + 128), f32),
        ] + [dma((nz,))] * 4 + [dma((nx, nz))] * 8 + [dma((ndev,))] * 4,
        compiler_params=pltpu.CompilerParams(
            collective_id=0, has_side_effects=True, vmem_limit_bytes=56 << 20
        ),
        name="gather_gram",
    )(cots, sources, energy)
    everything = everything.reshape(walkers, walkers + 128)
    gram = everything[:, :walkers]
    energies = everything[:, walkers]
    right_side = (energies - jnp.mean(energies)) * inv_root
    damped = gram + 0.01 * jnp.trace(gram) / walkers * jnp.eye(walkers, dtype=f32)
    weights = solve_damped(damped, right_side).astype(bf)
    return jnp.einsum("w,rwj->rj", weights, centered, preferred_element_type=f32)


def solution(mesh):
    lanes = ("groups", "wide", "pair", "cores")
    placed = (
        P(lanes, None, None),
        P(lanes, None, None),
        P(lanes, None, None, None),
        P(lanes),
    )
    return jax.shard_map(
        functools.partial(body, mesh.shape["wide"], mesh.shape["pair"]),
        mesh=mesh,
        in_specs=placed,
        out_specs=P(lanes, None),
        check_vma=False,
    )
```

time: 273 us -> 100 us (0.37)
  blocking collectives: 94.9 us -> 0 us
  waiting for transfers between devices: 84.9 us -> 0 us
  Pallas kernels: 0 us -> 59.7 us
  between operations: 15.5 us -> 1.39 us
  other arithmetic: 42.3 us -> 28.5 us
  local copies, waits for them, and re-layouts: 18.8 us -> 6.89 us
  starting transfers between devices: 7.58 us -> 0 us
  matrix products: 7.69 us -> 3.23 us
    unnamed x1 -> x0, blocking collectives: 94.9 us -> none
    psum x1 -> x0, waiting for transfers between devices: 84.9 us -> none  [body(): gram = lax.psum(partial_value, ('wide', 'pair', 'cores'))]
    pallas_call x0 -> x1, Pallas kernels: none -> 59.7 us  [body(): pl.pallas_call(functools.partial(gather_kernel, nz, nx, rows, elec, inv_r...]
    convert_element_type x2 -> x0, other arithmetic: 9.61 us -> none  [the longest x1 6.63 us: body(): flattened.astype(jnp.float32) - average]
    unnamed x14 -> x2, local copies, waits for them, and re-layouts: 10.4 us -> 1.85 us
    all_to_all x1 -> x0, starting transfers between devices: 7.54 us -> none  [body(): lax.all_to_all(grads, ('wide', 'pair', 'cores'), split_axis=1, concat_axi...]
    convert_element_type x2 -> x0, local copies, waits for them, and re-layouts: 4.58 us -> none  [the longest x1 3.99 us: body(): flattened.astype(jnp.float32) - average]
    dot_general x4 -> x1, matrix products: 7.34 us -> 2.88 us  [body(): jnp.einsum('w,rwj->rj', weights, centered, preferred_element_type=f32)]
  transfers between devices with their start and end apart: 2 -> 0, of which waited for: 1 -> 0; matrix products, arithmetic and copies ran while one was open for 6% -> 0% of each run, Pallas kernels for 0% -> 0%
where the time goes in v1:
time: 100 us; the launch traced here: 99.7 us
  Pallas kernels  59.7 us (60%)
  other arithmetic  28.5 us (28%)
  local copies, waits for them, and re-layouts  6.89 us (7%)
  matrix products  3.23 us (3%)
  between operations  1.39 us (1%)
    pallas_call x1, Pallas kernels, body(): pl.pallas_call(functools.partial(gather_kernel, nz, nx, rows, elec, inv_r...  59.7 us
    another operation x3, other arithmetic, solve_damped(): lower = jnp.linalg.cholesky(damped)  12.4 us
    another operation x2, other arithmetic, solve_damped(): jax.scipy.linalg.solve_triangular(lower, forward, lower=True, trans=1)  10.5 us
    dot_general x1, matrix products, body(): jnp.einsum('w,rwj->rj', weights, centered, preferred_element_type=f32)  2.88 us

profile of v1, /device:TPU:0, one launch (start us, length us, event | category | flops | bytes accessed | tf_op | source)
XLA Modules:
  0.0 99.7 jit_solution(7715201446141219111)
XLA Ops:
  0.0 1.3 %broadcast_in_dim.16.en_ref = f32[8,128]{1,0:T(8,128)} broadcast(f32[8]{0:T(128)} %param.7), dimensions={0} | broadcast | bytes 4128 | tf_op jit(solution)/shard_map/broadcast_in_dim | solution.py:239
  1.3 0.9 copy.7
  2.3 0.9 copy.8
  3.3 1.0 %copy.9 = bf16[1024,256]{1,0:T(8,128)(2,1)} copy(bf16[1024,256]{0,1:T(8,128)(2,1)S(1)} %fusion.3) | data formatting | bytes 1048576 | tf_op jit(solution)/shard_map/concatenate | solution.py:236
  4.3 1.9 %copy.10.c_ref = bf16[4,240,256]{2,1,0:T(8,128)(2,1)} copy(bf16[4,240,256]{2,0,1:T(4,128)(2,1)} %bitcast.44) | data formatting | bytes 983040 | tf_op jit(solution)/shard_map/reshape | solution.py:238
  6.2 59.7 %gather_gram.1 = (bf16[64,128,256]{2,1,0:T(8,128)(2,1)}, f32[16,8,256]{2,1,0:T(8,128)}) custom-call(bf16[4,240,256]{2,1,0:T(8,128)(2,1)} %copy.10.c_ref, bf16[16,64,256]{2,1,0:T(8,128)(2,1)} %bitcast.38, f32[8,128]{1,0:T(8,128)} %broadcast_in_dim.16.en_ref), custom_call_target="tpu_custom_call" | custom-call | tf_op jit(solution)/shard_map/gather_gram/pallas_call | solution.py:244
  66.0 1.5 %slice_reduce_fusion = f32[]{:T(128)} fusion(f32[128,256]{1,0:T(8,128)} %bitcast.39), kind=kLoop, calls=%fused_computation.20 | loop fusion | flops 127 | bytes 516 | tf_op jit(solution)/shard_map/reduce_sum | solution.py:270
  68.1 1.5 %select_reduce_fusion.1 = f32[]{:T(128)} fusion(f32[128,256]{1,0:T(8,128)} %bitcast.40), kind=kLoop, calls=%fused_computation.17 | loop fusion | flops 49151 | bytes 65540 | tf_op jit(solution)/shard_map/jit(trace)/reduce_sum | solution.py:271
  70.2 0.9 multiply_reduce_fusion
  71.1 0.9 select_add_fusion
  72.0 0.1 copy.11
  72.1 0.9 fusion.7
  73.0 11.7 %cholesky.17 = f32[128,128]{1,0:T(8,128)S(1)} custom-call(f32[128,128]{1,0:T(8,128)S(1)} %fusion.7), custom_call_target="Cholesky" | custom-call | tf_op jit(solution)/shard_map/jit(cholesky)/cholesky | solution.py:16
  84.7 0.6 compare_reduce_fusion
  85.3 0.7 fusion.4
  86.0 9.8 %custom-call.10 = f32[1,128,128]{1,2,0:T(8,128)S(1)} custom-call(f32[1,128,128]{2,1,0:T(8,128)S(1)} %fusion.4), custom_call_target="InvertDiagBlocksLowerTriangular" | custom-call | tf_op jit(solution)/shard_map/jit(_solve_triangular)/triangular_solve | solution.py:18
  95.8 0.2 convolution_bitcast_fusion.1
  96.0 0.2 fusion.1
  96.2 2.9 %fusion.9 = f32[1,64,256]{2,0,1:T(1,128)S(1)} fusion(bf16[128,1,1]{0,1,2:T(2,128)(2,1)S(1)} %fusion.1, bf16[64,128,256]{2,1,0:T(8,128)(2,1)} %get-tuple-element.8), kind=kOutput, calls=%fused_computation.23 | convolution fusion | flops 4194304 | bytes 4260096 | tf_op jit(solution)/shard_map/w,rwj->rj/dot_general | solution.py:273
  99.1 0.6 copy.14
  (5 shorter events, 0.2 us)

commit v2 on v1

--- a/solution.py
+++ b/solution.py
@@ -216,6 +216,64 @@
                 copy.wait_send()
         return unused
     lax.fori_loop(0, nz, s_left, 0)
+
+
+def solve_kernel(inv_root, all_ref, cent_ref, out_ref):
+    tiles, size, wide = all_ref.shape
+    walkers = tiles * size
+    lane = lax.broadcasted_iota(jnp.int32, (size, walkers), 1)
+    sub = lax.broadcasted_iota(jnp.int32, (size, walkers), 0)
+    a = [all_ref[i, :, 0:walkers] for i in range(tiles)]
+    e = [all_ref[i, :, walkers:wide] for i in range(tiles)]
+    diagonal = [lane == sub + size * i for i in range(tiles)]
+    picked = jnp.where(diagonal[0], a[0], 0.0)
+    total = e[0]
+    for i in range(1, tiles):
+        picked = picked + jnp.where(diagonal[i], a[i], 0.0)
+        total = total + e[i]
+    shift = 0.01 * jnp.sum(jnp.sum(picked, axis=0, keepdims=True), axis=1, keepdims=True) / walkers
+    average = jnp.sum(total, axis=0, keepdims=True) / walkers
+    y = [(e[i] - average) * inv_root for i in range(tiles)]
+    a = [a[i] + jnp.where(diagonal[i], shift, 0.0) for i in range(tiles)]
+
+    for k in range(tiles):
+        spread = [
+            [jnp.broadcast_to(a[i][:, size * k + j:size * k + j + 1], (size, walkers)) for j in range(size)]
+            for i in range(tiles)
+        ]
+        c = list(spread[k])
+        row, right = a[k], y[k]
+        scale = jnp.zeros((size, walkers), jnp.float32)
+        for j in range(size):
+            inverse = 1.0 / c[j][j:j + 1, :]
+            factor = jnp.where(sub == j, 0.0, c[j]) * inverse
+            for l in range(j + 1, size):
+                c[l] = c[l] - factor * c[l][j:j + 1, :]
+            row = row - factor * row[j:j + 1, :]
+            right = right - factor * right[j:j + 1, :]
+            scale = jnp.where(sub == j, inverse, scale)
+        row, right = row * scale, right * scale
+        a[k], y[k] = row, right
+        order = [(k + 1 + i) % tiles for i in range(tiles - 1)]
+        for i in order:
+            for j in range(size):
+                if k + 1 < tiles:
+                    a[i] = a[i] - spread[i][j] * row[j:j + 1, :]
+                y[i] = y[i] - spread[i][j] * right[j:j + 1, :]
+
+    weights = [v.astype(jnp.bfloat16).astype(jnp.float32) for v in y]
+    column = jnp.concatenate(weights, axis=0)
+    rows, _, width = cent_ref.shape
+    column = jnp.concatenate([column] * (width // walkers), axis=1)
+
+    def project(r, unused):
+        base = pl.multiple_of(r * 8, 8)
+        parts = [
+            jnp.sum(cent_ref[base + q].astype(jnp.float32) * column, axis=0, keepdims=True) for q in range(8)
+        ]
+        out_ref[pl.ds(base, 8), :] = jnp.concatenate(parts, axis=0)
+        return unused
+    lax.fori_loop(0, rows // 8, project, 0)
 
 
 def body(nz, nx, layer_input, mixed_heads, cotangents, local_energy):
@@ -264,6 +322,15 @@
         ),
         name="gather_gram",
     )(cots, sources, energy)
+    if walkers == 128:
+        return pl.pallas_call(
+            functools.partial(solve_kernel, inv_root),
+            out_shape=jax.ShapeDtypeStruct((rows, width), f32),
+            in_specs=[vmem] * 2,
+            out_specs=vmem,
+            compiler_params=pltpu.CompilerParams(vmem_limit_bytes=32 << 20),
+            name="solve_project",
+        )(everything, centered)
     everything = everything.reshape(walkers, walkers + 128)
     gram = everything[:, :walkers]
     energies = everything[:, walkers]

time: 100 us -> 77.5 us (0.78)
  other arithmetic: 28.5 us -> 0.04 us
  Pallas kernels: 59.7 us -> 67.9 us
  matrix products: 3.23 us -> 0 us
  local copies, waits for them, and re-layouts: 6.89 us -> 9.24 us
  between operations: 1.39 us -> 0.06 us
    another operation x5 -> x0, other arithmetic: 22.9 us -> none  [the longest x3 12.4 us: solve_damped(): lower = jnp.linalg.cholesky(damped)]
    pallas_call x0 -> x1, Pallas kernels: none -> 8.15 us  [body(): pl.pallas_call(functools.partial(solve_kernel, inv_root), out_shape=jax.S...]
    unnamed x2 -> x6, local copies, waits for them, and re-layouts: 1.85 us -> 4.94 us
    reduce_sum x2 -> x0, other arithmetic: 2.93 us -> none  [the longest x1 1.46 us: body(): jnp.trace(gram)]
    dot_general x1 -> x0, matrix products: 2.88 us -> none  [body(): jnp.einsum('w,rwj->rj', weights, centered, preferred_element_type=f32)]
where the time goes in v2:
time: 77.5 us; the launch traced here: 77.2 us
  Pallas kernels  67.9 us (88%)
  local copies, waits for them, and re-layouts  9.24 us (12%)
    pallas_call x1, Pallas kernels, body(): pl.pallas_call(functools.partial(gather_kernel, nz, nx, rows, elec, inv_r...  59.7 us
    pallas_call x1, Pallas kernels, body(): pl.pallas_call(functools.partial(solve_kernel, inv_root), out_shape=jax.S...  8.15 us
    unnamed x6, local copies, waits for them, and re-layouts  4.94 us
    reshape x1, local copies, waits for them, and re-layouts, body(): cots = jnp.swapaxes(cotangents, 0, 1).reshape(4, used, width)  1.9 us

profile of v2, /device:TPU:0, one launch (start us, length us, event | category | flops | bytes accessed | tf_op | source)
XLA Modules:
  0.0 77.2 jit_solution(17341809339589010467)
XLA Ops:
  0.0 1.3 %broadcast_in_dim.2.en_ref = f32[8,128]{1,0:T(8,128)} broadcast(f32[8]{0:T(128)} %param.7), dimensions={0} | broadcast | bytes 4128 | tf_op jit(solution)/shard_map/broadcast_in_dim | solution.py:297
  1.3 0.9 %copy.6 = bf16[8,30,256]{2,1,0:T(8,128)(2,1)S(1)} copy(bf16[8,30,256]{2,0,1:T(8,128)(2,1)} %param.4) | data formatting | bytes 245760 | tf_op args[0]
  2.3 0.9 %copy.7 = bf16[8,30,256]{2,1,0:T(8,128)(2,1)S(1)} copy(bf16[8,30,256]{2,0,1:T(8,128)(2,1)} %param.5) | data formatting | bytes 245760 | tf_op args[1]
  3.3 1.0 %copy.8 = bf16[1024,256]{1,0:T(8,128)(2,1)} copy(bf16[1024,256]{0,1:T(8,128)(2,1)S(1)} %fusion.1) | data formatting | bytes 1048576 | tf_op jit(solution)/shard_map/concatenate | solution.py:294
  4.3 1.9 %copy.9.c_ref = bf16[4,240,256]{2,1,0:T(8,128)(2,1)} copy(bf16[4,240,256]{2,0,1:T(4,128)(2,1)} %bitcast.7) | data formatting | bytes 983040 | tf_op jit(solution)/shard_map/reshape | solution.py:296
  6.2 59.7 %gather_gram.1 = (bf16[64,128,256]{2,1,0:T(8,128)(2,1)}, f32[16,8,256]{2,1,0:T(8,128)}) custom-call(bf16[4,240,256]{2,1,0:T(8,128)(2,1)} %copy.9.c_ref, bf16[16,64,256]{2,1,0:T(8,128)(2,1)} %bitcast.6, f32[8,128]{1,0:T(8,128)} %broadcast_in_dim.2.en_ref), custom_call_target="tpu_custom_call" | custom-call | tf_op jit(solution)/shard_map/gather_gram/pallas_call | solution.py:302
  66.0 0.0 copy-start
  66.0 2.2 %copy-done = bf16[64,128,256]{2,1,0:T(8,128)(2,1)S(1)} copy-done((bf16[64,128,256]{2,1,0:T(8,128)(2,1)S(1)}, bf16[64,128,256]{2,1,0:T(8,128)(2,1)}, u32[]{:S(2)}) %copy-start) | copy-done | bytes 4194328
  68.1 0.0 copy-start.1
  68.1 0.9 %copy-done.1 = f32[16,8,256]{2,1,0:T(8,128)S(1)} copy-done((f32[16,8,256]{2,1,0:T(8,128)S(1)}, f32[16,8,256]{2,1,0:T(8,128)}, u32[]{:S(2)}) %copy-start.1) | copy-done | bytes 131096
  69.0 8.2 %solve_project.1 = f32[64,256]{1,0:T(8,128)} custom-call(f32[16,8,256]{2,1,0:T(8,128)S(1)} %copy-done.1, bf16[64,128,256]{2,1,0:T(8,128)(2,1)S(1)} %copy-done), custom_call_target="tpu_custom_call" | custom-call | tf_op jit(solution)/shard_map/solve_project/pallas_call | solution.py:326
  (4 shorter events, 0.1 us)
Async XLA Ops:
  66.0 2.2 %copy-start = (bf16[64,128,256]{2,1,0:T(8,128)(2,1)S(1)}, bf16[64,128,256]{2,1,0:T(8,128)(2,1)}, u32[]{:S(2)}) copy-start(bf16[64,128,256]{2,1,0:T(8,128)(2,1)} %get-tuple-element.8.cent_ref) | copy-start | bytes 12582916
  68.1 0.9 %copy-start.1 = (f32[16,8,256]{2,1,0:T(8,128)S(1)}, f32[16,8,256]{2,1,0:T(8,128)}, u32[]{:S(2)}) copy-start(f32[16,8,256]{2,1,0:T(8,128)} %get-tuple-element.7.all_ref) | copy-start | bytes 393220

commit v3 on v2

--- a/solution.py
+++ b/solution.py
@@ -19,9 +19,9 @@
 
 
 def gather_kernel(
-    nz, nx, rows, elec, inv_root,
-    c_ref, st_ref, en_ref, cent_ref, gall_ref,
-    cbuf, sz, sx, sbuf, grads, gpart, rbuf, gbuf,
+    nz, nx, rows, inv_root,
+    layer_ref, heads_ref, cot_ref, en_ref, cent_ref, gall_ref,
+    c_ref, st_ref, turn, cbuf, sz, sx, sbuf, grads, gpart, rbuf, gbuf,
     zs_c, zr_c, zs_s, zr_s, xs_c, xr_c, xs_s, xr_s, cs_c, cr_c, cs_s, cr_s,
     gs, gr, hs, hr,
 ):
@@ -30,7 +30,6 @@
     ndev = nz * nx * nc
     sib = 1 - c
     me = (z * nx + x) * nc + c
-    used = c_ref.shape[1]
     depth = cbuf.shape[1]
     width = cbuf.shape[2]
     walk = ndev * 8
@@ -38,11 +37,6 @@
     def dev(d):
         return (g, d // (nx * nc), (d // nc) % nx, d % nc)
 
-    def clear(o, unused):
-        cbuf[o, used:depth, :] = jnp.zeros((depth - used, width), cbuf.dtype)
-        return unused
-    lax.fori_loop(0, ndev, clear, 0)
-
     barrier = pltpu.get_barrier_semaphore()
 
     def greet(k, unused):
@@ -50,6 +44,24 @@
         pl.semaphore_signal(barrier, inc=1, device_id=dev(d), device_id_type=MESH)
         return unused
     lax.fori_loop(1, ndev, greet, 0)
+
+    elec = layer_ref.shape[1]
+    slot_rows = depth // 8
+    c_ref[...] = jnp.zeros_like(c_ref)
+    for w in range(8):
+        for m in range(4):
+            c_ref[m, w * slot_rows:w * slot_rows + elec, :] = cot_ref[w, m]
+    turn[...] = jnp.zeros_like(turn)
+    slabs = width // rows
+    for source, first_slab, times in ((layer_ref, 0, 3), (heads_ref, 3 * slabs, 1)):
+        for w in range(8):
+            turn[w * slot_rows:w * slot_rows + elec, :] = source[w].astype(jnp.float32)
+        turned = turn[...].T.astype(jnp.bfloat16).reshape(slabs, rows, depth)
+        for again in range(times):
+            at = first_slab + again * slabs
+            st_ref[at:at + slabs, 0:rows, :] = turned
+    if st_ref.shape[1] > rows:
+        st_ref[:, rows:, :] = jnp.zeros((ndev, st_ref.shape[1] - rows, depth), jnp.bfloat16)
     pl.semaphore_wait(barrier, ndev - 1)
 
     def origin(s, xx, cc):
@@ -60,7 +72,7 @@
         o = origin(src_z, x, c)
         return (
             pltpu.make_async_remote_copy(
-                c_ref.at[m], cbuf.at[o, pl.ds(0, used)], zs_c.at[dz], zr_c.at[src_z],
+                c_ref.at[m], cbuf.at[o], zs_c.at[dz], zr_c.at[src_z],
                 device_id=(g, zt, x, c), device_id_type=MESH),
             pltpu.make_async_remote_copy(
                 st_ref.at[pl.ds(zt * nx * nc, nx * nc)], sz.at[src_z], zs_s.at[dz], zr_s.at[src_z],
@@ -71,7 +83,7 @@
         o = origin(s, xo, c)
         return (
             pltpu.make_async_remote_copy(
-                cbuf.at[o, pl.ds(0, used)], cbuf.at[o, pl.ds(0, used)], xs_c.at[dx, s], xr_c.at[xo, s],
+                cbuf.at[o], cbuf.at[o], xs_c.at[dx, s], xr_c.at[xo, s],
                 device_id=(g, z, xt, c), device_id_type=MESH),
             pltpu.make_async_remote_copy(
                 sz.at[s, pl.ds(xt * nc, nc)], sx.at[xo, s], xs_s.at[dx, s], xr_s.at[xo, s],
@@ -82,25 +94,34 @@
         o = origin(s, xo, co)
         return (
             pltpu.make_async_remote_copy(
-                cbuf.at[o, pl.ds(0, used)], cbuf.at[o, pl.ds(0, used)], cs_c.at[xo, s], cr_c.at[xo, s],
+                cbuf.at[o], cbuf.at[o], cs_c.at[xo, s], cr_c.at[xo, s],
                 device_id=(g, z, x, sib), device_id_type=MESH),
             pltpu.make_async_remote_copy(
                 src, sbuf.at[o], cs_s.at[xo, s], cr_s.at[xo, s],
                 device_id=(g, z, x, sib), device_id_type=MESH),
         )
 
-    def z_send(dz, unused):
-        for copy in z_copies(lax.rem(z + dz, nz), z, dz):
-            copy.start()
-        return unused
-    lax.fori_loop(1, nz, z_send, 0)
-
-    cbuf[me, 0:used, :] = c_ref[(4 * z) // nz]
+    half = nz // 2
+
+    def offset(t):
+        away = jnp.where(lax.rem(t, 2) == 0, half - t // 2, half + t // 2)
+        return jnp.where(t == 0, 0, away)
+
+    def z_round(t):
+        return z_copies(lax.rem(z + offset(t), nz), z, t)
+
+    def z_from(t):
+        return lax.rem(z + nz - offset(t), nz)
+
+    for copy in z_round(1):
+        copy.start()
+
+    cbuf[me] = c_ref[(4 * z) // nz]
     sz[z] = st_ref[pl.ds(z * nx * nc, nx * nc)]
 
     slot = lax.broadcasted_iota(jnp.int32, (8, depth), 1)
     walker = lax.broadcasted_iota(jnp.int32, (8, depth), 0)
-    own = (slot >= walker * elec) & (slot < walker * elec + elec)
+    own = (slot >= walker * slot_rows) & (slot < (walker + 1) * slot_rows)
     step = min(rows, 16)
 
     def form(p):
@@ -121,7 +142,13 @@
     def pipeline(t, unused):
         @pl.when(t < nz)
         def first():
-            s = lax.rem(z + nz - t, nz)
+            s = z_from(t)
+
+            @pl.when((t > 0) & (t < nz - 1))
+            def onward():
+                for copy, later in zip(z_round(t), z_round(t + 1)):
+                    copy.wait_send()
+                    later.start()
 
             @pl.when(t > 0)
             def arrived():
@@ -136,7 +163,7 @@
 
         @pl.when((t >= 1) & (t < nz + 1))
         def second():
-            s = lax.rem(z + nz - t + 1, nz)
+            s = z_from(t - 1)
             for dx in range(1, nx):
                 xo = lax.rem(x + nx - dx, nx)
                 for copy in x_copies(s, xo, x, 0):
@@ -147,7 +174,7 @@
 
         @pl.when(t >= 2)
         def third():
-            s = lax.rem(z + nz - t + 2, nz)
+            s = z_from(t - 2)
             for dx in range(nx):
                 xo = lax.rem(x + nx - dx, nx)
                 for copy in c_copies(s, xo, sib, sz.at[s, 0]):
@@ -173,7 +200,7 @@
                                   preferred_element_type=jnp.float32)
             gpart[r * 16:(r + 1) * 16] += add.reshape(16, 8, walk)
         return unused
-    lax.fori_loop(0, rows // batch, share, 0)
+    lax.fori_loop(0, rows // batch, share, 0, unroll=2)
 
     def g_copy(src_d, dst_d, k):
         return pltpu.make_async_remote_copy(
@@ -193,7 +220,11 @@
     rbuf[me] = gpart[me]
     each(lambda k: g_copy(lax.rem(me + k, ndev), me, k).wait_recv())
     gbuf[me, :, 0:walk] = jnp.sum(rbuf[...], axis=0)
-    gbuf[me, :, walk:walk + 128] = en_ref[...]
+    energy = jnp.zeros((8, 128), jnp.float32)
+    place = lax.broadcasted_iota(jnp.int32, (8, 128), 0)
+    for w in range(8):
+        energy = jnp.where(place == w, en_ref[w], energy)
+    gbuf[me, :, walk:walk + 128] = energy
     each(lambda k: h_copy(me, lax.rem(me + k, ndev), k).start())
     each(lambda k: h_copy(lax.rem(me + k, ndev), me, k).wait_recv())
     gall_ref[...] = gbuf[...]
@@ -201,11 +232,8 @@
     each(lambda k: g_copy(me, lax.rem(me + k, ndev), k).wait_send())
     each(lambda k: h_copy(me, lax.rem(me + k, ndev), k).wait_send())
 
-    def z_left(dz, unused):
-        for copy in z_copies(lax.rem(z + dz, nz), z, dz):
-            copy.wait_send()
-        return unused
-    lax.fori_loop(1, nz, z_left, 0)
+    for copy in z_round(nz - 1):
+        copy.wait_send()
 
     def s_left(s, unused):
         for dx in range(1, nx):
@@ -284,30 +312,23 @@
     inv_root = 1.0 / math.sqrt(walkers)
     rows = 4 * width // ndev
     rows_held = max(rows, 16)
-    used = walk_dev * elec
-    depth = -(-used // 128) * 128
-
-    def turned(source):
-        return jnp.pad(source.reshape(used, width).T, ((0, 0), (0, depth - used)))
-
-    layer = turned(layer_input)
-    sources = jnp.concatenate([layer, layer, layer, turned(mixed_heads)], axis=0).reshape(ndev, rows, depth)
-    sources = jnp.pad(sources, ((0, 0), (0, rows_held - rows), (0, 0)))
-    cots = jnp.swapaxes(cotangents, 0, 1).reshape(4, used, width)
-    energy = jnp.broadcast_to(local_energy[:, None], (walk_dev, 128))
+    depth = walk_dev * (-(-elec // 16) * 16)
 
     bf, f32 = jnp.bfloat16, jnp.float32
     dma = pltpu.SemaphoreType.DMA
     vmem = pl.BlockSpec(memory_space=pltpu.VMEM)
     centered, everything = pl.pallas_call(
-        functools.partial(gather_kernel, nz, nx, rows, elec, inv_root),
+        functools.partial(gather_kernel, nz, nx, rows, inv_root),
         out_shape=(
             jax.ShapeDtypeStruct((rows, walkers, width), bf),
             jax.ShapeDtypeStruct((ndev, walk_dev, walkers + 128), f32),
         ),
-        in_specs=[vmem] * 3,
+        in_specs=[vmem] * 3 + [pl.BlockSpec(memory_space=pltpu.SMEM)],
         out_specs=(vmem, vmem),
         scratch_shapes=[
+            pltpu.VMEM((4, depth, width), bf),
+            pltpu.VMEM((ndev, rows_held, depth), bf),
+            pltpu.VMEM((depth, width), f32),
             pltpu.VMEM((ndev, depth, width), bf),
             pltpu.VMEM((nz, nx * nc, rows_held, depth), bf),
             pltpu.VMEM((nx, nz, nc, rows_held, depth), bf),
@@ -321,7 +342,7 @@
             collective_id=0, has_side_effects=True, vmem_limit_bytes=56 << 20
         ),
         name="gather_gram",
-    )(cots, sources, energy)
+    )(layer_input, mixed_heads, cotangents, local_energy)
     if walkers == 128:
         return pl.pallas_call(
             functools.partial(solve_kernel, inv_root),

time: 77.5 us -> 75.1 us (0.969)
  Pallas kernels: 67.9 us -> 66.6 us
  local copies, waits for them, and re-layouts: 9.24 us -> 8.15 us
    unnamed x6 -> x7, local copies, waits for them, and re-layouts: 4.94 us -> 8.15 us
    reshape x3 -> x0, local copies, waits for them, and re-layouts: 1.98 us -> none  [the longest x1 1.9 us: body(): cots = jnp.swapaxes(cotangents, 0, 1).reshape(4, used, width)]
    broadcast_in_dim x1 -> x0, local copies, waits for them, and re-layouts: 1.31 us -> none  [body(): energy = jnp.broadcast_to(local_energy[:, None], (walk_dev, 128))]
    pallas_call x1, Pallas kernels: 59.7 us -> 58.5 us  [body(): pl.pallas_call(functools.partial(gather_kernel, nz, nx, rows, inv_root),...]
    concatenate x1 -> x0, local copies, waits for them, and re-layouts: 1 us -> none  [body(): jnp.concatenate([layer, layer, layer, turned(mixed_heads)], axis=0)]
where the time goes in v3:
time: 75.1 us; the launch traced here: 74.8 us
  Pallas kernels  66.6 us (89%)
  local copies, waits for them, and re-layouts  8.15 us (11%)
    pallas_call x1, Pallas kernels, body(): pl.pallas_call(functools.partial(gather_kernel, nz, nx, rows, inv_root),...  58.5 us
    unnamed x7, local copies, waits for them, and re-layouts  8.15 us
    pallas_call x1, Pallas kernels, body(): pl.pallas_call(functools.partial(solve_kernel, inv_root), out_shape=jax.S...  8.15 us

profile of v3, /device:TPU:0, one launch (start us, length us, event | category | flops | bytes accessed | tf_op | source)
XLA Modules:
  0.0 74.8 jit_solution(5372415791590004583)
XLA Ops:
  0.0 1.6 %copy.5.layer_ref = bf16[8,30,256]{2,1,0:T(8,128)(2,1)} copy(bf16[8,30,256]{2,0,1:T(8,128)(2,1)} %param.4) | data formatting | bytes 245760 | tf_op args[0]
  1.6 1.6 %copy.6.heads_ref = bf16[8,30,256]{2,1,0:T(8,128)(2,1)} copy(bf16[8,30,256]{2,0,1:T(8,128)(2,1)} %param.5) | data formatting | bytes 245760 | tf_op args[1]
  3.2 1.9 %copy.7.cot_ref = bf16[8,4,30,256]{3,2,1,0:T(8,128)(2,1)} copy(bf16[8,4,30,256]{3,1,2,0:T(4,128)(2,1)} %param.6) | data formatting | bytes 983040 | tf_op args[2]
  5.1 58.5 %gather_gram.1 = (bf16[64,128,256]{2,1,0:T(8,128)(2,1)}, f32[16,8,256]{2,1,0:T(8,128)}) custom-call(bf16[8,30,256]{2,1,0:T(8,128)(2,1)} %copy.5.layer_ref, bf16[8,30,256]{2,1,0:T(8,128)(2,1)} %copy.6.heads_ref, bf16[8,4,30,256]{3,2,1,0:T(8,128)(2,1)} %copy.7.cot_ref, f32[8]{0:T(128)} %en_ref.1), custom_call_target="tpu_custom_call" | custom-call | tf_op jit(solution)/shard_map/gather_gram/pallas_call | solution.py:320
  63.5 0.0 copy-start
  63.5 2.2 %copy-done = bf16[64,128,256]{2,1,0:T(8,128)(2,1)S(1)} copy-done((bf16[64,128,256]{2,1,0:T(8,128)(2,1)S(1)}, bf16[64,128,256]{2,1,0:T(8,128)(2,1)}, u32[]{:S(2)}) %copy-start) | copy-done | bytes 4194328
  65.7 0.0 copy-start.1
  65.7 0.9 %copy-done.1 = f32[16,8,256]{2,1,0:T(8,128)S(1)} copy-done((f32[16,8,256]{2,1,0:T(8,128)S(1)}, f32[16,8,256]{2,1,0:T(8,128)}, u32[]{:S(2)}) %copy-start.1) | copy-done | bytes 131096
  66.6 8.2 %solve_project.1 = f32[64,256]{1,0:T(8,128)} custom-call(f32[16,8,256]{2,1,0:T(8,128)S(1)} %copy-done.1, bf16[64,128,256]{2,1,0:T(8,128)(2,1)S(1)} %copy-done), custom_call_target="tpu_custom_call" | custom-call | tf_op jit(solution)/shard_map/solve_project/pallas_call | solution.py:347
Async XLA Ops:
  63.5 2.2 %copy-start = (bf16[64,128,256]{2,1,0:T(8,128)(2,1)S(1)}, bf16[64,128,256]{2,1,0:T(8,128)(2,1)}, u32[]{:S(2)}) copy-start(bf16[64,128,256]{2,1,0:T(8,128)(2,1)} %get-tuple-element.8.cent_ref) | copy-start | bytes 12582916
  65.7 0.9 %copy-start.1 = (f32[16,8,256]{2,1,0:T(8,128)S(1)}, f32[16,8,256]{2,1,0:T(8,128)}, u32[]{:S(2)}) copy-start(f32[16,8,256]{2,1,0:T(8,128)} %get-tuple-element.7.all_ref) | copy-start | bytes 393220

commit v4 on v3

--- a/solution.py
+++ b/solution.py
@@ -20,8 +20,8 @@
 
 def gather_kernel(
     nz, nx, rows, inv_root,
-    layer_ref, heads_ref, cot_ref, en_ref, cent_ref, gall_ref,
-    c_ref, st_ref, turn, cbuf, sz, sx, sbuf, grads, gpart, rbuf, gbuf,
+    layer_ref, heads_ref, c_ref, en_ref, cent_ref, gall_ref,
+    st_ref, cbuf, sz, sx, sbuf, grads, gpart, rbuf, gbuf,
     zs_c, zr_c, zs_s, zr_s, xs_c, xr_c, xs_s, xr_s, cs_c, cr_c, cs_s, cr_s,
     gs, gr, hs, hr,
 ):
@@ -43,25 +43,21 @@
         d = lax.rem(me + k, ndev)
         pl.semaphore_signal(barrier, inc=1, device_id=dev(d), device_id_type=MESH)
         return unused
-    lax.fori_loop(1, ndev, greet, 0)
-
-    elec = layer_ref.shape[1]
-    slot_rows = depth // 8
-    c_ref[...] = jnp.zeros_like(c_ref)
-    for w in range(8):
-        for m in range(4):
-            c_ref[m, w * slot_rows:w * slot_rows + elec, :] = cot_ref[w, m]
-    turn[...] = jnp.zeros_like(turn)
+    lax.fori_loop(1, ndev, greet, 0, unroll=ndev <= 16)
+
+    used = c_ref.shape[1]
+
+    def clear(o, unused):
+        cbuf[o, used:depth, :] = jnp.zeros((depth - used, width), cbuf.dtype)
+        return unused
+    lax.fori_loop(0, ndev, clear, 0)
+    st_ref[...] = jnp.zeros_like(st_ref)
     slabs = width // rows
     for source, first_slab, times in ((layer_ref, 0, 3), (heads_ref, 3 * slabs, 1)):
-        for w in range(8):
-            turn[w * slot_rows:w * slot_rows + elec, :] = source[w].astype(jnp.float32)
-        turned = turn[...].T.astype(jnp.bfloat16).reshape(slabs, rows, depth)
+        turned = source[...].astype(jnp.float32).T.astype(jnp.bfloat16).reshape(slabs, rows, used)
         for again in range(times):
             at = first_slab + again * slabs
-            st_ref[at:at + slabs, 0:rows, :] = turned
-    if st_ref.shape[1] > rows:
-        st_ref[:, rows:, :] = jnp.zeros((ndev, st_ref.shape[1] - rows, depth), jnp.bfloat16)
+            st_ref[at:at + slabs, 0:rows, 0:used] = turned
     pl.semaphore_wait(barrier, ndev - 1)
 
     def origin(s, xx, cc):
@@ -70,20 +66,22 @@
     def z_copies(zt, src_z, dz):
         m = (4 * zt) // nz
         o = origin(src_z, x, c)
-        return (
-            pltpu.make_async_remote_copy(
-                c_ref.at[m], cbuf.at[o], zs_c.at[dz], zr_c.at[src_z],
-                device_id=(g, zt, x, c), device_id_type=MESH),
-            pltpu.make_async_remote_copy(
-                st_ref.at[pl.ds(zt * nx * nc, nx * nc)], sz.at[src_z], zs_s.at[dz], zr_s.at[src_z],
-                device_id=(g, zt, x, c), device_id_type=MESH),
-        )
+        copies = [pltpu.make_async_remote_copy(
+            c_ref.at[m], cbuf.at[o, pl.ds(0, used)], zs_c.at[dz], zr_c.at[src_z],
+            device_id=(g, zt, x, c), device_id_type=MESH)]
+        for dx in range(1, nx + 1):
+            xt = lax.rem(x + dx, nx)
+            copies.append(pltpu.make_async_remote_copy(
+                st_ref.at[pl.ds((zt * nx + xt) * nc, nc)], sz.at[src_z, pl.ds(xt * nc, nc)],
+                zs_s.at[dx - 1, dz], zr_s.at[dx - 1, src_z],
+                device_id=(g, zt, x, c), device_id_type=MESH))
+        return copies
 
     def x_copies(s, xo, xt, dx):
         o = origin(s, xo, c)
         return (
             pltpu.make_async_remote_copy(
-                cbuf.at[o], cbuf.at[o], xs_c.at[dx, s], xr_c.at[xo, s],
+                cbuf.at[o, pl.ds(0, used)], cbuf.at[o, pl.ds(0, used)], xs_c.at[dx, s], xr_c.at[xo, s],
                 device_id=(g, z, xt, c), device_id_type=MESH),
             pltpu.make_async_remote_copy(
                 sz.at[s, pl.ds(xt * nc, nc)], sx.at[xo, s], xs_s.at[dx, s], xr_s.at[xo, s],
@@ -94,7 +92,7 @@
         o = origin(s, xo, co)
         return (
             pltpu.make_async_remote_copy(
-                cbuf.at[o], cbuf.at[o], cs_c.at[xo, s], cr_c.at[xo, s],
+                cbuf.at[o, pl.ds(0, used)], cbuf.at[o, pl.ds(0, used)], cs_c.at[xo, s], cr_c.at[xo, s],
                 device_id=(g, z, x, sib), device_id_type=MESH),
             pltpu.make_async_remote_copy(
                 src, sbuf.at[o], cs_s.at[xo, s], cr_s.at[xo, s],
@@ -113,15 +111,15 @@
     def z_from(t):
         return lax.rem(z + nz - offset(t), nz)
 
-    for copy in z_round(1):
+    for copy in z_round(1) + z_round(2)[:1]:
         copy.start()
 
-    cbuf[me] = c_ref[(4 * z) // nz]
+    cbuf[me, 0:used, :] = c_ref[(4 * z) // nz]
     sz[z] = st_ref[pl.ds(z * nx * nc, nx * nc)]
 
     slot = lax.broadcasted_iota(jnp.int32, (8, depth), 1)
     walker = lax.broadcasted_iota(jnp.int32, (8, depth), 0)
-    own = (slot >= walker * slot_rows) & (slot < (walker + 1) * slot_rows)
+    own = lax.rem(slot, 8) == walker
     step = min(rows, 16)
 
     def form(p):
@@ -144,21 +142,27 @@
         def first():
             s = z_from(t)
 
-            @pl.when((t > 0) & (t < nz - 1))
-            def onward():
-                for copy, later in zip(z_round(t), z_round(t + 1)):
-                    copy.wait_send()
-                    later.start()
-
-            @pl.when(t > 0)
-            def arrived():
-                for copy in z_copies(z, s, 0):
-                    copy.wait_recv()
+            def land(j):
+                @pl.when(t > 0)
+                def arrived():
+                    z_round(t)[j].wait_send()
+                    ahead = 1 if j < nx else 2
+
+                    @pl.when(t + ahead < nz)
+                    def onward():
+                        z_round(t + ahead)[(j + 1) % (nx + 1)].start()
+                    z_copies(z, s, 0)[j].wait_recv()
+
+            to_sib = c_copies(s, x, c, sz.at[s, x * nc + sib])
+            land(0)
             for dx in range(1, nx):
-                for copy in x_copies(s, x, lax.rem(x + dx, nx), dx):
-                    copy.start()
-            for copy in c_copies(s, x, c, sz.at[s, x * nc + sib]):
-                copy.start()
+                x_copies(s, x, lax.rem(x + dx, nx), dx)[0].start()
+            to_sib[0].start()
+            for dx in range(1, nx):
+                land(dx)
+                x_copies(s, x, lax.rem(x + dx, nx), dx)[1].start()
+            land(nx)
+            to_sib[1].start()
             sbuf[origin(s, x, c)] = sz[s, x * nc + c]
 
         @pl.when((t >= 1) & (t < nz + 1))
@@ -166,10 +170,9 @@
             s = z_from(t - 1)
             for dx in range(1, nx):
                 xo = lax.rem(x + nx - dx, nx)
-                for copy in x_copies(s, xo, x, 0):
+                for copy, onward in zip(x_copies(s, xo, x, 0), c_copies(s, xo, c, sx.at[xo, s, sib])):
                     copy.wait_recv()
-                for copy in c_copies(s, xo, c, sx.at[xo, s, sib]):
-                    copy.start()
+                    onward.start()
                 sbuf[origin(s, xo, c)] = sx[xo, s, c]
 
         @pl.when(t >= 2)
@@ -214,7 +217,7 @@
         def run(k, unused):
             fn(k)
             return unused
-        lax.fori_loop(1, ndev, run, 0)
+        lax.fori_loop(1, ndev, run, 0, unroll=ndev <= 16)
 
     each(lambda k: g_copy(me, lax.rem(me + k, ndev), k).start())
     rbuf[me] = gpart[me]
@@ -232,8 +235,6 @@
     each(lambda k: g_copy(me, lax.rem(me + k, ndev), k).wait_send())
     each(lambda k: h_copy(me, lax.rem(me + k, ndev), k).wait_send())
 
-    for copy in z_round(nz - 1):
-        copy.wait_send()
 
     def s_left(s, unused):
         for dx in range(1, nx):
@@ -312,7 +313,11 @@
     inv_root = 1.0 / math.sqrt(walkers)
     rows = 4 * width // ndev
     rows_held = max(rows, 16)
-    depth = walk_dev * (-(-elec // 16) * 16)
+    used = elec * walk_dev
+    depth = -(-used // 128) * 128
+    layer_rows = jnp.swapaxes(layer_input, 0, 1).reshape(used, width)
+    heads_rows = jnp.swapaxes(mixed_heads, 0, 1).reshape(used, width)
+    cots = jnp.transpose(cotangents, (1, 2, 0, 3)).reshape(4, used, width)
 
     bf, f32 = jnp.bfloat16, jnp.float32
     dma = pltpu.SemaphoreType.DMA
@@ -326,9 +331,7 @@
         in_specs=[vmem] * 3 + [pl.BlockSpec(memory_space=pltpu.SMEM)],
         out_specs=(vmem, vmem),
         scratch_shapes=[
-            pltpu.VMEM((4, depth, width), bf),
             pltpu.VMEM((ndev, rows_held, depth), bf),
-            pltpu.VMEM((depth, width), f32),
             pltpu.VMEM((ndev, depth, width), bf),
             pltpu.VMEM((nz, nx * nc, rows_held, depth), bf),
             pltpu.VMEM((nx, nz, nc, rows_held, depth), bf),
@@ -337,19 +340,19 @@
             pltpu.VMEM((ndev, walk_dev, walkers), f32),
             pltpu.VMEM((ndev, walk_dev, walkers), f32),
             pltpu.VMEM((ndev, walk_dev, walkers + 128), f32),
-        ] + [dma((nz,))] * 4 + [dma((nx, nz))] * 8 + [dma((ndev,))] * 4,
+        ] + [dma((nz,))] * 2 + [dma((nx, nz))] * 10 + [dma((ndev,))] * 4,
         compiler_params=pltpu.CompilerParams(
-            collective_id=0, has_side_effects=True, vmem_limit_bytes=56 << 20
+            collective_id=0, has_side_effects=True, vmem_limit_bytes=(24 if ndev <= 16 else 56) << 20
         ),
         name="gather_gram",
-    )(layer_input, mixed_heads, cotangents, local_energy)
+    )(layer_rows, heads_rows, cots, local_energy)
     if walkers == 128:
         return pl.pallas_call(
             functools.partial(solve_kernel, inv_root),
             out_shape=jax.ShapeDtypeStruct((rows, width), f32),
             in_specs=[vmem] * 2,
             out_specs=vmem,
-            compiler_params=pltpu.CompilerParams(vmem_limit_bytes=32 << 20),
+            compiler_params=pltpu.CompilerParams(vmem_limit_bytes=16 << 20),
             name="solve_project",
         )(everything, centered)
     everything = everything.reshape(walkers, walkers + 128)

time: 75.1 us -> 63.5 us (0.85)
  Pallas kernels: 66.6 us -> 59.7 us
  local copies, waits for them, and re-layouts: 8.15 us -> 3.58 us
    pallas_call x1, Pallas kernels: 58.5 us -> 51.5 us  [body(): pl.pallas_call(functools.partial(gather_kernel, nz, nx, rows, inv_root),...]
    unnamed x7 -> x6, local copies, waits for them, and re-layouts: 8.15 us -> 2.45 us
    transpose x0 -> x1, local copies, waits for them, and re-layouts: none -> 1.12 us  [body(): cots = jnp.transpose(cotangents, (1, 2, 0, 3)).reshape(4, used, width)]
where the time goes in v4:
time: 63.5 us; the launch traced here: 63.3 us
  Pallas kernels  59.7 us (94%)
  local copies, waits for them, and re-layouts  3.58 us (6%)
    pallas_call x1, Pallas kernels, body(): pl.pallas_call(functools.partial(gather_kernel, nz, nx, rows, inv_root),...  51.5 us
    pallas_call x1, Pallas kernels, body(): pl.pallas_call(functools.partial(solve_kernel, inv_root), out_shape=jax.S...  8.16 us
    unnamed x6, local copies, waits for them, and re-layouts  2.45 us

profile of v4, /device:TPU:0, one launch (start us, length us, event | category | flops | bytes accessed | tf_op | source)
XLA Modules:
  0.0 63.3 jit_solution(17221484853789819420)
XLA Ops:
  0.0 1.1 %copy.7 = bf16[4,30,8,256]{3,2,1,0:T(8,128)(2,1)S(1)} copy(bf16[4,30,8,256]{3,0,1,2:T(4,128)(2,1)} %bitcast.13) | data formatting | bytes 983040 | tf_op jit(solution)/shard_map/transpose | solution.py:320
  1.1 0.0 copy-start
  1.1 0.9 %copy-done = bf16[8,30,256]{2,0,1:T(8,128)(2,1)S(1)} copy-done((bf16[8,30,256]{2,0,1:T(8,128)(2,1)S(1)}, bf16[8,30,256]{2,0,1:T(8,128)(2,1)}, u32[]{:S(2)}) %copy-start) | copy-done | bytes 122904
  2.0 0.0 copy-start.1
  2.0 0.9 %copy-done.1 = bf16[8,30,256]{2,0,1:T(8,128)(2,1)S(1)} copy-done((bf16[8,30,256]{2,0,1:T(8,128)(2,1)S(1)}, bf16[8,30,256]{2,0,1:T(8,128)(2,1)}, u32[]{:S(2)}) %copy-start.1) | copy-done | bytes 122904
  2.9 0.0 copy-start.2
  2.9 0.7 %copy-done.2 = f32[8]{0:T(128)S(1)} copy-done((f32[8]{0:T(128)S(1)}, f32[8]{0:T(128)}, u32[]{:S(2)}) %copy-start.2) | copy-done | bytes 56
  3.6 51.5 %gather_gram.1 = (bf16[64,128,256]{2,1,0:T(8,128)(2,1)S(1)}, f32[16,8,256]{2,1,0:T(8,128)S(1)}) custom-call(bf16[240,256]{1,0:T(8,128)(2,1)S(1)} %bitcast.11, bf16[240,256]{1,0:T(8,128)(2,1)S(1)} %bitcast.12, bf16[4,240,256]{2,1,0:T(8,128)(2,1)S(1)} %bitcast.10, f32[8]{0:T(128)S(1)} %copy-done.2), custom_call_target="tpu_custom_call" | custom-call | tf_op jit(solution)/shard_map/gather_gram/pallas_call | solution.py:325
  55.1 8.2 %solve_project.1 = f32[64,256]{1,0:T(8,128)} custom-call(f32[16,8,256]{2,1,0:T(8,128)S(1)} %get-tuple-element.7.all_ref, bf16[64,128,256]{2,1,0:T(8,128)(2,1)S(1)} %get-tuple-element.8.cent_ref), custom_call_target="tpu_custom_call" | custom-call | tf_op jit(solution)/shard_map/solve_project/pallas_call | solution.py:350
Async XLA Ops:
  1.1 0.9 %copy-start = (bf16[8,30,256]{2,0,1:T(8,128)(2,1)S(1)}, bf16[8,30,256]{2,0,1:T(8,128)(2,1)}, u32[]{:S(2)}) copy-start(bf16[8,30,256]{2,0,1:T(8,128)(2,1)} %param.4) | copy-start | bytes 368644
  2.0 0.9 %copy-start.1 = (bf16[8,30,256]{2,0,1:T(8,128)(2,1)S(1)}, bf16[8,30,256]{2,0,1:T(8,128)(2,1)}, u32[]{:S(2)}) copy-start(bf16[8,30,256]{2,0,1:T(8,128)(2,1)} %param.5) | copy-start | bytes 368644
  2.9 0.7 %copy-start.2 = (f32[8]{0:T(128)S(1)}, f32[8]{0:T(128)}, u32[]{:S(2)}) copy-start(f32[8]{0:T(128)} %en_ref.1) | copy-start | bytes 100

commit v5 on v4

--- a/solution.py
+++ b/solution.py
@@ -138,6 +138,15 @@
         lax.fori_loop(0, rows // step, part, 0)
 
     def pipeline(t, unused):
+        @pl.when(t >= 2)
+        def third():
+            s = z_from(t - 2)
+            for dx in range(nx):
+                xo = lax.rem(x + nx - dx, nx)
+                for copy in c_copies(s, xo, sib, sz.at[s, 0]):
+                    copy.wait_recv()
+                form(s * nx + xo)
+
         @pl.when(t < nz)
         def first():
             s = z_from(t)
@@ -174,15 +183,6 @@
                     copy.wait_recv()
                     onward.start()
                 sbuf[origin(s, xo, c)] = sx[xo, s, c]
-
-        @pl.when(t >= 2)
-        def third():
-            s = z_from(t - 2)
-            for dx in range(nx):
-                xo = lax.rem(x + nx - dx, nx)
-                for copy in c_copies(s, xo, sib, sz.at[s, 0]):
-                    copy.wait_recv()
-                form(s * nx + xo)
         return unused
     lax.fori_loop(0, nz + 2, pipeline, 0)
 
@@ -203,7 +203,7 @@
                                   preferred_element_type=jnp.float32)
             gpart[r * 16:(r + 1) * 16] += add.reshape(16, 8, walk)
         return unused
-    lax.fori_loop(0, rows // batch, share, 0, unroll=2)
+    lax.fori_loop(0, rows // batch, share, 0, unroll=4 if ndev <= 16 else 1)
 
     def g_copy(src_d, dst_d, k):
         return pltpu.make_async_remote_copy(
@@ -286,9 +286,12 @@
         order = [(k + 1 + i) % tiles for i in range(tiles - 1)]
         for i in order:
             for j in range(size):
-                if k + 1 < tiles:
-                    a[i] = a[i] - spread[i][j] * row[j:j + 1, :]
-                y[i] = y[i] - spread[i][j] * right[j:j + 1, :]
+                a[i] = a[i] - spread[i][j] * row[j:j + 1, :]
+                if k == 0:
+                    y[i] = y[i] - spread[i][j] * right[j:j + 1, :]
+        if k == 0:
+            a = [jnp.where(lane == 0, y[i], a[i]) for i in range(tiles)]
+    y = [jnp.broadcast_to(a[i][:, 0:1], (size, walkers)) for i in range(tiles)]
 
     weights = [v.astype(jnp.bfloat16).astype(jnp.float32) for v in y]
     column = jnp.concatenate(weights, axis=0)

time: 63.5 us -> 62.9 us (level)
    pallas_call x1, Pallas kernels: 51.5 us -> 50.9 us  [body(): pl.pallas_call(functools.partial(gather_kernel, nz, nx, rows, inv_root),...]
where the time goes in v5:
time: 62.9 us; the launch traced here: 62.7 us
  Pallas kernels  59.1 us (94%)
  local copies, waits for them, and re-layouts  3.58 us (6%)
    pallas_call x1, Pallas kernels, body(): pl.pallas_call(functools.partial(gather_kernel, nz, nx, rows, inv_root),...  50.9 us
    pallas_call x1, Pallas kernels, body(): pl.pallas_call(functools.partial(solve_kernel, inv_root), out_shape=jax.S...  8.2 us
    unnamed x6, local copies, waits for them, and re-layouts  2.45 us

profile of v5, /device:TPU:0, one launch (start us, length us, event | category | flops | bytes accessed | tf_op | source)
XLA Modules:
  0.0 62.7 jit_solution(5706831588759777694)
XLA Ops:
  0.0 1.1 %copy.7 = bf16[4,30,8,256]{3,2,1,0:T(8,128)(2,1)S(1)} copy(bf16[4,30,8,256]{3,0,1,2:T(4,128)(2,1)} %bitcast.13) | data formatting | bytes 983040 | tf_op jit(solution)/shard_map/transpose | solution.py:323
  1.1 0.0 copy-start
  1.1 0.9 %copy-done = bf16[8,30,256]{2,0,1:T(8,128)(2,1)S(1)} copy-done((bf16[8,30,256]{2,0,1:T(8,128)(2,1)S(1)}, bf16[8,30,256]{2,0,1:T(8,128)(2,1)}, u32[]{:S(2)}) %copy-start) | copy-done | bytes 122904
  2.0 0.0 copy-start.1
  2.0 0.9 %copy-done.1 = bf16[8,30,256]{2,0,1:T(8,128)(2,1)S(1)} copy-done((bf16[8,30,256]{2,0,1:T(8,128)(2,1)S(1)}, bf16[8,30,256]{2,0,1:T(8,128)(2,1)}, u32[]{:S(2)}) %copy-start.1) | copy-done | bytes 122904
  2.9 0.0 copy-start.2
  2.9 0.7 %copy-done.2 = f32[8]{0:T(128)S(1)} copy-done((f32[8]{0:T(128)S(1)}, f32[8]{0:T(128)}, u32[]{:S(2)}) %copy-start.2) | copy-done | bytes 56
  3.6 50.9 %gather_gram.1 = (bf16[64,128,256]{2,1,0:T(8,128)(2,1)S(1)}, f32[16,8,256]{2,1,0:T(8,128)S(1)}) custom-call(bf16[240,256]{1,0:T(8,128)(2,1)S(1)} %bitcast.11, bf16[240,256]{1,0:T(8,128)(2,1)S(1)} %bitcast.12, bf16[4,240,256]{2,1,0:T(8,128)(2,1)S(1)} %bitcast.10, f32[8]{0:T(128)S(1)} %copy-done.2), custom_call_target="tpu_custom_call" | custom-call | tf_op jit(solution)/shard_map/gather_gram/pallas_call | solution.py:328
  54.5 8.2 %solve_project.1 = f32[64,256]{1,0:T(8,128)} custom-call(f32[16,8,256]{2,1,0:T(8,128)S(1)} %get-tuple-element.7.all_ref, bf16[64,128,256]{2,1,0:T(8,128)(2,1)S(1)} %get-tuple-element.8.cent_ref), custom_call_target="tpu_custom_call" | custom-call | tf_op jit(solution)/shard_map/solve_project/pallas_call | solution.py:353
Async XLA Ops:
  1.1 0.9 %copy-start = (bf16[8,30,256]{2,0,1:T(8,128)(2,1)S(1)}, bf16[8,30,256]{2,0,1:T(8,128)(2,1)}, u32[]{:S(2)}) copy-start(bf16[8,30,256]{2,0,1:T(8,128)(2,1)} %param.4) | copy-start | bytes 368644
  2.0 0.9 %copy-start.1 = (bf16[8,30,256]{2,0,1:T(8,128)(2,1)S(1)}, bf16[8,30,256]{2,0,1:T(8,128)(2,1)}, u32[]{:S(2)}) copy-start(bf16[8,30,256]{2,0,1:T(8,128)(2,1)} %param.5) | copy-start | bytes 368644
  2.9 0.7 %copy-start.2 = (f32[8]{0:T(128)S(1)}, f32[8]{0:T(128)}, u32[]{:S(2)}) copy-start(f32[8]{0:T(128)} %en_ref.1) | copy-start | bytes 100

commit v6 on v5

--- a/solution.py
+++ b/solution.py
@@ -135,7 +135,7 @@
             both = jnp.concatenate(halves, axis=1).astype(jnp.bfloat16)
             grads[pl.ds(base, step), pl.ds(pl.multiple_of(p * 16, 16), 16), :] = both
             return unused
-        lax.fori_loop(0, rows // step, part, 0)
+        lax.fori_loop(0, rows // step, part, 0, unroll=True)
 
     def pipeline(t, unused):
         @pl.when(t >= 2)

time: 62.9 us -> 62 us (0.986)
  Pallas kernels: 59.1 us -> 58.2 us
    pallas_call x1, Pallas kernels: 50.9 us -> 50 us  [body(): pl.pallas_call(functools.partial(gather_kernel, nz, nx, rows, inv_root),...]
where the time goes in v6:
time: 62 us; the launch traced here: 61.8 us
  Pallas kernels  58.2 us (94%)
  local copies, waits for them, and re-layouts  3.58 us (6%)
    pallas_call x1, Pallas kernels, body(): pl.pallas_call(functools.partial(gather_kernel, nz, nx, rows, inv_root),...  50 us
    pallas_call x1, Pallas kernels, body(): pl.pallas_call(functools.partial(solve_kernel, inv_root), out_shape=jax.S...  8.2 us
    unnamed x6, local copies, waits for them, and re-layouts  2.45 us

profile of v6, /device:TPU:0, one launch (start us, length us, event | category | flops | bytes accessed | tf_op | source)
XLA Modules:
  0.0 61.8 jit_solution(16844106504808719609)
XLA Ops:
  0.0 1.1 %copy.7 = bf16[4,30,8,256]{3,2,1,0:T(8,128)(2,1)S(1)} copy(bf16[4,30,8,256]{3,0,1,2:T(4,128)(2,1)} %bitcast.13) | data formatting | bytes 983040 | tf_op jit(solution)/shard_map/transpose | solution.py:323
  1.1 0.0 copy-start
  1.1 0.9 %copy-done = bf16[8,30,256]{2,0,1:T(8,128)(2,1)S(1)} copy-done((bf16[8,30,256]{2,0,1:T(8,128)(2,1)S(1)}, bf16[8,30,256]{2,0,1:T(8,128)(2,1)}, u32[]{:S(2)}) %copy-start) | copy-done | bytes 122904
  2.0 0.0 copy-start.1
  2.0 0.9 %copy-done.1 = bf16[8,30,256]{2,0,1:T(8,128)(2,1)S(1)} copy-done((bf16[8,30,256]{2,0,1:T(8,128)(2,1)S(1)}, bf16[8,30,256]{2,0,1:T(8,128)(2,1)}, u32[]{:S(2)}) %copy-start.1) | copy-done | bytes 122904
  2.9 0.0 copy-start.2
  2.9 0.7 %copy-done.2 = f32[8]{0:T(128)S(1)} copy-done((f32[8]{0:T(128)S(1)}, f32[8]{0:T(128)}, u32[]{:S(2)}) %copy-start.2) | copy-done | bytes 56
  3.6 50.0 %gather_gram.1 = (bf16[64,128,256]{2,1,0:T(8,128)(2,1)S(1)}, f32[16,8,256]{2,1,0:T(8,128)S(1)}) custom-call(bf16[240,256]{1,0:T(8,128)(2,1)S(1)} %bitcast.11, bf16[240,256]{1,0:T(8,128)(2,1)S(1)} %bitcast.12, bf16[4,240,256]{2,1,0:T(8,128)(2,1)S(1)} %bitcast.10, f32[8]{0:T(128)S(1)} %copy-done.2), custom_call_target="tpu_custom_call" | custom-call | tf_op jit(solution)/shard_map/gather_gram/pallas_call | solution.py:328
  53.6 8.2 %solve_project.1 = f32[64,256]{1,0:T(8,128)} custom-call(f32[16,8,256]{2,1,0:T(8,128)S(1)} %get-tuple-element.7.all_ref, bf16[64,128,256]{2,1,0:T(8,128)(2,1)S(1)} %get-tuple-element.8.cent_ref), custom_call_target="tpu_custom_call" | custom-call | tf_op jit(solution)/shard_map/solve_project/pallas_call | solution.py:353
Async XLA Ops:
  1.1 0.9 %copy-start = (bf16[8,30,256]{2,0,1:T(8,128)(2,1)S(1)}, bf16[8,30,256]{2,0,1:T(8,128)(2,1)}, u32[]{:S(2)}) copy-start(bf16[8,30,256]{2,0,1:T(8,128)(2,1)} %param.4) | copy-start | bytes 368644
  2.0 0.9 %copy-start.1 = (bf16[8,30,256]{2,0,1:T(8,128)(2,1)S(1)}, bf16[8,30,256]{2,0,1:T(8,128)(2,1)}, u32[]{:S(2)}) copy-start(bf16[8,30,256]{2,0,1:T(8,128)(2,1)} %param.5) | copy-start | bytes 368644
  2.9 0.7 %copy-start.2 = (f32[8]{0:T(128)S(1)}, f32[8]{0:T(128)}, u32[]{:S(2)}) copy-start(f32[8]{0:T(128)} %en_ref.1) | copy-start | bytes 100
